TPU v7x, 512 devices: a whole 4x4x16 slice. The times are simulated.
512 devices in a mesh: dp: 8 (over z_lo), block: 64 (over x, z_hi, y, core).
Axes of the slice: x: 4, y: 4, z: 16 (z_hi: 2, z_lo: 8; z = z_hi * 8 + z_lo), core: 2. Of those that a mesh axis runs over, the one named last changes fastest.
Arguments:
- features_in: bfloat16 [2048, 65536], P('dp', 'block'), may hold values from -6 to 6
- cotangent: bfloat16 [2048, 65536], P('dp', 'block'), may hold values from -6 to 6
- left_one: bfloat16 [256, 256, 256], P('block'), may hold values from -0.375 to 0.375
- right_one: bfloat16 [256, 256, 256], P('block'), may hold values from -0.375 to 0.375
- left_two: bfloat16 [256, 256, 256], P('block'), may hold values from -0.375 to 0.375
- right_two: bfloat16 [256, 256, 256], P('block'), may hold values from -0.375 to 0.375
Outputs:
- input_grad: bfloat16 [2048, 65536], P('dp', 'block')
- left_one_grad: float32 [256, 256, 256], P('dp', 'block')
- right_one_grad: float32 [256, 256, 256], P('dp', 'block')
- left_two_grad: float32 [256, 256, 256], P('dp', 'block')
- right_two_grad: float32 [256, 256, 256], P('dp', 'block')
All inputs are finite; a program needn't handle non-finite values.
Results may differ from a plain program's by a relative error of at most 0.017.
Values may be sent and summed in bfloat16 or wider, within the bound.
A program may use at most 64 MiB of HBM per device.

v0:
```python
import jax
import jax.numpy as jnp
from jax import lax
from jax.sharding import PartitionSpec as P


def gelu_tanh(values):
    return jax.nn.gelu(values, approximate=True)


def turned(values):
    return jnp.swapaxes(values, 1, 2)


def grad_term(cot_part, act_part, form, factor_scale):

    def compute(offset, amount):
        return (
            jnp.einsum(form, cot_part, act_part, preferred_element_type=jnp.float32) * factor_scale
        )

    return compute


def per_device(features_in, cotangent, left_one, right_one, left_two, right_two):
    f32 = jnp.float32
    bf16 = jnp.bfloat16
    tok_rows = features_in.shape[0]
    local_blocks = left_one.shape[0]
    block_size = left_one.shape[1]
    factor_scale = float(tok_rows * lax.axis_size("dp")) ** (-0.5)
    inputs3 = features_in.reshape(tok_rows, local_blocks, block_size)
    cot3 = cotangent.reshape(tok_rows, local_blocks, block_size)
    first_out = jnp.einsum("tji,jmi->tjm", inputs3, left_one, preferred_element_type=f32).astype(
        bf16
    )
    first_cols = lax.all_to_all(turned(first_out), "block", split_axis=1, concat_axis=2, tiled=True)
    mixed_one = jnp.einsum(
        "tki,kmi->tkm", first_cols, right_one, preferred_element_type=f32
    ).astype(bf16)
    hidden = lax.all_to_all(turned(mixed_one), "block", split_axis=1, concat_axis=2, tiled=True)
    hidden32 = hidden.astype(f32)
    activated = gelu_tanh(hidden32).astype(bf16)
    second_out = jnp.einsum("tji,jmi->tjm", activated, left_two, preferred_element_type=f32).astype(
        bf16
    )
    second_cols = lax.all_to_all(
        turned(second_out), "block", split_axis=1, concat_axis=2, tiled=True
    )
    cot_cols = lax.all_to_all(turned(cot3), "block", split_axis=1, concat_axis=2, tiled=True)
    pairs = []
    pairs.append(grad_term(cot_cols, second_cols, "tkm,tki->mki", factor_scale))
    back_two = jnp.einsum("tkm,kmi->tki", cot_cols, right_two, preferred_element_type=f32).astype(
        bf16
    )
    back_rows = lax.all_to_all(turned(back_two), "block", split_axis=1, concat_axis=2, tiled=True)
    pairs.append(grad_term(back_rows, activated, "tjm,tji->mji", factor_scale))
    grad_act = jnp.einsum("tjm,jmi->tji", back_rows, left_two, preferred_element_type=f32)
    _, pullback = jax.vjp(gelu_tanh, hidden32)
    grad_hidden = pullback(grad_act)[0].astype(bf16)
    hidden_cols = lax.all_to_all(
        turned(grad_hidden), "block", split_axis=1, concat_axis=2, tiled=True
    )
    pairs.append(grad_term(hidden_cols, first_cols, "tkm,tki->mki", factor_scale))
    back_one = jnp.einsum(
        "tkm,kmi->tki", hidden_cols, right_one, preferred_element_type=f32
    ).astype(bf16)
    first_rows = lax.all_to_all(turned(back_one), "block", split_axis=1, concat_axis=2, tiled=True)
    pairs.append(grad_term(first_rows, inputs3, "tjm,tji->mji", factor_scale))
    input_grad = jnp.einsum(
        "tjm,jmi->tji", first_rows, left_one, preferred_element_type=f32
    ).astype(bf16)
    input_grad = input_grad.reshape(tok_rows, local_blocks * block_size)
    terms = [compute(0, block_size) for compute in pairs]
    right_two_grad, left_two_grad, right_one_grad, left_one_grad = (
        lax.psum_scatter(
            terms[0].astype(jnp.bfloat16), "dp", scatter_dimension=0, tiled=True
        ).astype(jnp.float32),
        lax.psum_scatter(
            terms[1].astype(jnp.bfloat16), "dp", scatter_dimension=0, tiled=True
        ).astype(jnp.float32),
        lax.psum_scatter(
            terms[2].astype(jnp.bfloat16), "dp", scatter_dimension=0, tiled=True
        ).astype(jnp.float32),
        lax.psum_scatter(
            terms[3].astype(jnp.bfloat16), "dp", scatter_dimension=0, tiled=True
        ).astype(jnp.float32),
    )
    return (input_grad, left_one_grad, right_one_grad, left_two_grad, right_two_grad)


def solution(mesh):
    return jax.shard_map(
        per_device,
        mesh=mesh,
        in_specs=(
            P("dp", "block"),
            P("dp", "block"),
            P("block", None, None),
            P("block", None, None),
            P("block", None, None),
            P("block", None, None),
        ),
        out_specs=(
            P("dp", "block"),
            P("dp", "block", None),
            P("dp", "block", None),
            P("dp", "block", None),
            P("dp", "block", None),
        ),
        check_vma=False,
    )
```

profile of v0, /device:TPU:6, one launch (start us, length us, event | category | flops | bytes accessed | tf_op | source)
XLA Modules:
  0.0 449.9 jit_solution(6929397058265165811)
XLA Ops:
  7.2 1.6 fusion.9
  8.8 1.2 copy.75
  10.0 21.6 %all-to-all-start.2 = ((bf16[256,256,4]{0,2,1:T(4,128)(2,1)}), bf16[256,256,4]{0,2,1:T(4,128)(2,1)S(1)}, u32[]{:S(2)}, u32[]{:S(2)}) async-start(bf16[256,256,4]{0,2,1:T(4,128)(2,1)} %copy.75), calls=%async_computation.2 | async-start | bytes 1048576 | tf_op jit(solution)/shard_map/all_to_all | solution.py:37
  31.9 1.3 copy.67
  33.2 18.1 %all-to-all-done.2 = bf16[256,256,4]{0,2,1:T(4,128)(2,1)S(1)} async-done(((bf16[256,256,4]{0,2,1:T(4,128)(2,1)}), bf16[256,256,4]{0,2,1:T(4,128)(2,1)S(1)}, u32[]{:S(2)}, u32[]{:S(2)}) %all-to-all-start.2) | async-done | bytes 524320 | tf_op jit(solution)/shard_map/all_to_all | solution.py:37
  51.3 6.6 %all-to-all-start = ((bf16[256,256,4]{0,2,1:T(4,128)(2,1)}), bf16[256,256,4]{0,2,1:T(4,128)(2,1)S(1)}, u32[]{:S(2)}, u32[]{:S(2)}) async-start(bf16[256,256,4]{0,2,1:T(4,128)(2,1)} %bitcast), calls=%async_computation | async-start | bytes 1048576 | tf_op jit(solution)/shard_map/all_to_all | solution.py:50
  60.3 16.7 %all-to-all-done = bf16[256,256,4]{0,2,1:T(4,128)(2,1)S(1)} async-done(((bf16[256,256,4]{0,2,1:T(4,128)(2,1)}), bf16[256,256,4]{0,2,1:T(4,128)(2,1)S(1)}, u32[]{:S(2)}, u32[]{:S(2)}) %all-to-all-start) | async-done | bytes 524320 | tf_op jit(solution)/shard_map/all_to_all | solution.py:50
  77.1 8.2 %all-to-all-start.3 = ((bf16[256,256,4]{0,2,1:T(4,128)(2,1)}), bf16[256,256,4]{0,2,1:T(4,128)(2,1)S(1)}, u32[]{:S(2)}, u32[]{:S(2)}) async-start(bf16[256,256,4]{0,2,1:T(4,128)(2,1)} %copy.78), calls=%async_computation.3 | async-start | bytes 1048576 | tf_op jit(solution)/shard_map/all_to_all | solution.py:41
  85.8 1.4 fusion.8
  87.2 1.2 copy.71
  88.5 16.0 %all-to-all-done.3 = bf16[256,256,4]{0,2,1:T(4,128)(2,1)S(1)} async-done(((bf16[256,256,4]{0,2,1:T(4,128)(2,1)}), bf16[256,256,4]{0,2,1:T(4,128)(2,1)S(1)}, u32[]{:S(2)}, u32[]{:S(2)}) %all-to-all-start.3) | async-done | bytes 524320 | tf_op jit(solution)/shard_map/all_to_all | solution.py:41
  104.5 13.4 %all-to-all-start.1 = ((bf16[256,256,4]{0,2,1:T(4,128)(2,1)}), bf16[256,256,4]{0,2,1:T(4,128)(2,1)}, u32[]{:S(2)}, u32[]{:S(2)}) async-start(bf16[256,256,4]{0,2,1:T(4,128)(2,1)} %copy.71), calls=%async_computation.1 | async-start | bytes 1048576 | tf_op jit(solution)/shard_map/all_to_all | solution.py:56
  118.5 1.4 copy.83
  119.9 17.2 %all-to-all-done.1 = bf16[256,256,4]{0,2,1:T(4,128)(2,1)} async-done(((bf16[256,256,4]{0,2,1:T(4,128)(2,1)}), bf16[256,256,4]{0,2,1:T(4,128)(2,1)}, u32[]{:S(2)}, u32[]{:S(2)}) %all-to-all-start.1) | async-done | bytes 524320 | tf_op jit(solution)/shard_map/all_to_all | solution.py:56
  137.0 1.2 copy.72
  138.6 2.3 fusion.20
  142.0 10.9 %all-to-all-start.4 = ((bf16[256,256,4]{0,2,1:T(4,128)(2,1)}), bf16[256,256,4]{0,2,1:T(4,128)(2,1)S(1)}, u32[]{:S(2)}, u32[]{:S(2)}) async-start(bf16[256,256,4]{0,2,1:T(4,128)(2,1)} %copy.85), calls=%async_computation.4 | async-start | bytes 1048576 | tf_op jit(solution)/shard_map/all_to_all | solution.py:61
  152.9 1.7 fusion.12
  155.7 16.4 %all-to-all-done.4 = bf16[256,256,4]{0,2,1:T(4,128)(2,1)S(1)} async-done(((bf16[256,256,4]{0,2,1:T(4,128)(2,1)}), bf16[256,256,4]{0,2,1:T(4,128)(2,1)S(1)}, u32[]{:S(2)}, u32[]{:S(2)}) %all-to-all-start.4) | async-done | bytes 524320 | tf_op jit(solution)/shard_map/all_to_all | solution.py:61
  172.1 22.2 %all-to-all-start.6 = ((bf16[256,256,4]{0,2,1:T(4,128)(2,1)}), bf16[256,256,4]{0,2,1:T(4,128)(2,1)}, u32[]{:S(2)}, u32[]{:S(2)}) async-start(bf16[256,256,4]{0,2,1:T(4,128)(2,1)} %copy.101), calls=%async_computation.7 | async-start | bytes 1048576 | tf_op jit(solution)/shard_map/all_to_all | solution.py:47
  196.2 25.2 %all-to-all-done.6 = bf16[256,256,4]{0,2,1:T(4,128)(2,1)} async-done(((bf16[256,256,4]{0,2,1:T(4,128)(2,1)}), bf16[256,256,4]{0,2,1:T(4,128)(2,1)}, u32[]{:S(2)}, u32[]{:S(2)}) %all-to-all-start.6) | async-done | bytes 524320 | tf_op jit(solution)/shard_map/all_to_all | solution.py:47
  221.4 15.5 %all-to-all-start.5 = ((bf16[256,256,4]{0,2,1:T(4,128)(2,1)}), bf16[256,256,4]{0,2,1:T(4,128)(2,1)}, u32[]{:S(2)}, u32[]{:S(2)}) async-start(bf16[256,256,4]{0,2,1:T(4,128)(2,1)} %copy.88), calls=%async_computation.5 | async-start | bytes 1048576 | tf_op jit(solution)/shard_map/all_to_all | solution.py:68
  236.9 1.8 fusion.5
  239.8 1.2 copy.102
  244.0 12.0 %all-to-all-done.5 = bf16[256,256,4]{0,2,1:T(4,128)(2,1)} async-done(((bf16[256,256,4]{0,2,1:T(4,128)(2,1)}), bf16[256,256,4]{0,2,1:T(4,128)(2,1)}, u32[]{:S(2)}, u32[]{:S(2)}) %all-to-all-start.5) | async-done | bytes 524320 | tf_op jit(solution)/shard_map/all_to_all | solution.py:68
  256.0 1.3 copy.89
  258.5 1.3 dynamic-slice
  260.4 118.0 %all-reduce.6.cloned.1.call-done = (bf16[256,4,256]{2,1,0:T(4,128)(2,1)}, bf16[256,4,256]{2,1,0:T(4,128)(2,1)}, bf16[256,4,256]{2,1,0:T(4,128)(2,1)}) async-done(((bf16[256,4,256]{2,1,0:T(4,128)(2,1)}, bf16[256,4,256]{2,1,0:T(4,128)(2,1)}, bf16[256,4,256]{2,1,0:T(4,128)(2,1)}), (bf16[256,4,256]{2,1,0:T(4,128)(2,1)}, bf16[256,4,256]{2,1,0:T(4,128)(2,1)}, ...) | async-done | bytes 1572880
  378.4 1.5 dynamic-slice_convert_fusion.2
  379.9 1.6 dynamic-slice_convert_fusion
  382.9 58.7 %reduce-scatter.2.cloned.1.call-done = bf16[32,4,256]{2,0,1:T(8,128)(2,1)} async-done(((bf16[256,4,256]{2,0,1:T(8,128)(2,1)}), bf16[32,4,256]{2,0,1:T(8,128)(2,1)}) %reduce-scatter.2.cloned.1.call-update) | async-done | bytes 65552 | tf_op jit(solution)/shard_map/reduce_scatter | solution.py:85
  441.5 1.5 copy.106
  (42 shorter events, 14.8 us)
Async XLA Ops:
  7.2 131.4 %copy-start = (bf16[4,256,256]{2,1,0:T(8,128)(2,1)S(1)}, bf16[4,256,256]{2,1,0:T(8,128)(2,1)}, u32[]{:S(2)}) copy-start(bf16[4,256,256]{2,1,0:T(8,128)(2,1)} %param.10) | copy-start | bytes 1572868
  10.0 21.6 %copy-start.4 = (bf16[256,1024]{1,0:T(8,128)(2,1)S(1)}, bf16[256,1024]{1,0:T(8,128)(2,1)}, u32[]{:S(2)}) copy-start(bf16[256,1024]{1,0:T(8,128)(2,1)} %param.7) | copy-start | bytes 1572868
  10.0 41.3 %all-to-all-start.2 = ((bf16[256,256,4]{0,2,1:T(4,128)(2,1)}), bf16[256,256,4]{0,2,1:T(4,128)(2,1)S(1)}, u32[]{:S(2)}, u32[]{:S(2)}) async-start(bf16[256,256,4]{0,2,1:T(4,128)(2,1)} %copy.75), calls=%async_computation.2 | async-start | bytes 1048576 | tf_op jit(solution)/shard_map/all_to_all | solution.py:37
  51.3 25.8 %all-to-all-start = ((bf16[256,256,4]{0,2,1:T(4,128)(2,1)}), bf16[256,256,4]{0,2,1:T(4,128)(2,1)S(1)}, u32[]{:S(2)}, u32[]{:S(2)}) async-start(bf16[256,256,4]{0,2,1:T(4,128)(2,1)} %bitcast), calls=%async_computation | async-start | bytes 1048576 | tf_op jit(solution)/shard_map/all_to_all | solution.py:50
  57.9 1.0 copy-start.1
  77.1 27.4 %all-to-all-start.3 = ((bf16[256,256,4]{0,2,1:T(4,128)(2,1)}), bf16[256,256,4]{0,2,1:T(4,128)(2,1)S(1)}, u32[]{:S(2)}, u32[]{:S(2)}) async-start(bf16[256,256,4]{0,2,1:T(4,128)(2,1)} %copy.78), calls=%async_computation.3 | async-start | bytes 1048576 | tf_op jit(solution)/shard_map/all_to_all | solution.py:41
  104.5 32.5 %all-to-all-start.1 = ((bf16[256,256,4]{0,2,1:T(4,128)(2,1)}), bf16[256,256,4]{0,2,1:T(4,128)(2,1)}, u32[]{:S(2)}, u32[]{:S(2)}) async-start(bf16[256,256,4]{0,2,1:T(4,128)(2,1)} %copy.71), calls=%async_computation.1 | async-start | bytes 1048576 | tf_op jit(solution)/shard_map/all_to_all | solution.py:56
  138.6 2.3 copy-start.5
  142.0 30.2 %all-to-all-start.4 = ((bf16[256,256,4]{0,2,1:T(4,128)(2,1)}), bf16[256,256,4]{0,2,1:T(4,128)(2,1)S(1)}, u32[]{:S(2)}, u32[]{:S(2)}) async-start(bf16[256,256,4]{0,2,1:T(4,128)(2,1)} %copy.85), calls=%async_computation.4 | async-start | bytes 1048576 | tf_op jit(solution)/shard_map/all_to_all | solution.py:61
  172.1 49.3 %all-to-all-start.6 = ((bf16[256,256,4]{0,2,1:T(4,128)(2,1)}), bf16[256,256,4]{0,2,1:T(4,128)(2,1)}, u32[]{:S(2)}, u32[]{:S(2)}) async-start(bf16[256,256,4]{0,2,1:T(4,128)(2,1)} %copy.101), calls=%async_computation.7 | async-start | bytes 1048576 | tf_op jit(solution)/shard_map/all_to_all | solution.py:47
  196.2 40.7 %copy-start.6 = (bf16[256,4,256]{2,0,1:T(8,128)(2,1)S(1)}, bf16[256,4,256]{2,0,1:T(8,128)(2,1)}, u32[]{:S(2)}) copy-start(bf16[256,4,256]{2,0,1:T(8,128)(2,1)} %copy-done.5) | copy-start | bytes 1572868
  221.4 34.6 %all-to-all-start.5 = ((bf16[256,256,4]{0,2,1:T(4,128)(2,1)}), bf16[256,256,4]{0,2,1:T(4,128)(2,1)}, u32[]{:S(2)}, u32[]{:S(2)}) async-start(bf16[256,256,4]{0,2,1:T(4,128)(2,1)} %copy.88), calls=%async_computation.5 | async-start | bytes 1048576 | tf_op jit(solution)/shard_map/all_to_all | solution.py:68
  236.9 141.5 %all-reduce.6.cloned.1.call-start = ((), (), s32[]{:S(2)}) async-start(), calls=%async_computation.9 | async-start | bytes 3145728
  243.9 197.6 %reduce-scatter.2.cloned.1.call-start = ((), (), s32[]{:S(2)}) async-start(), calls=%async_computation.8 | async-start | bytes 589824 | tf_op jit(solution)/shard_map/reduce_scatter | solution.py:85
  256.0 1.3 copy-start.3
  258.4 123.1 %copy-start.2 = (bf16[4,256,256]{2,1,0:T(8,128)(2,1)S(1)}, bf16[4,256,256]{2,1,0:T(8,128)(2,1)}, u32[]{:S(2)}) copy-start(bf16[4,256,256]{2,1,0:T(8,128)(2,1)} %param.8) | copy-start | bytes 1572868
Sparse Core Ops, SparseCore 0:
  244.0 134.3 all-reduce.5
  381.2 60.2 reduce-scatter.1
where the time goes:
time: 451 us; the launch traced here: 450 us
  waiting for transfers between devices  298 us (66%)
  starting transfers between devices  98.4 us (22%)
  local copies, waits for them, and re-layouts  23.4 us (5%)
  between operations  15 us (3%)
  matrix products  11.4 us (3%)
    unnamed x3, waiting for transfers between devices  118 us
    reduce_scatter x1, waiting for transfers between devices, per_device(): lax.psum_scatter(terms[3].astype(jnp.bfloat16), 'dp', scatter_dimension=0...  58.7 us
    all_to_all x1, waiting for transfers between devices, per_device(): lax.all_to_all(turned(second_out), 'block', split_axis=1, concat_axis=2,...  25.2 us
    all_to_all x1, starting transfers between devices, per_device(): lax.all_to_all(turned(second_out), 'block', split_axis=1, concat_axis=2,...  22.2 us
    all_to_all x1, starting transfers between devices, per_device(): lax.all_to_all(turned(first_out), 'block', split_axis=1, concat_axis=2, t...  21.6 us
    all_to_all x1, waiting for transfers between devices, per_device(): lax.all_to_all(turned(first_out), 'block', split_axis=1, concat_axis=2, t...  18.1 us
    all_to_all x1, waiting for transfers between devices, per_device(): lax.all_to_all(turned(back_two), 'block', split_axis=1, concat_axis=2, ti...  17.2 us
    all_to_all x1, waiting for transfers between devices, per_device(): lax.all_to_all(turned(cot3), 'block', split_axis=1, concat_axis=2, tiled=...  16.7 us
  transfers between devices with their start and end apart: 9, of which 9 were waited for; matrix products, arithmetic and copies ran while one was open for 6% of the time, Pallas kernels for 0%

commit v1 on v0

v1 whole, which is shorter than its diff:
```python
import jax
import jax.numpy as jnp
from jax import lax
from jax.experimental import pallas as pl
from jax.experimental.pallas import tpu as pltpu
from jax.sharding import PartitionSpec as P

MESH = pl.DeviceIdType.MESH
F32 = jnp.float32
BF16 = jnp.bfloat16
SIZE = 256
TOK = 128
PLANE = 32
NN = ((1,), (0,))
NT = ((1,), (1,))
TN = ((0,), (0,))


def dot(a, b, dims):
    return lax.dot_general(a, b, (dims, ((), ())), preferred_element_type=F32)


def selection(place):
    row = lax.broadcasted_iota(jnp.int32, (SIZE, SIZE), 0)
    col = lax.broadcasted_iota(jnp.int32, (SIZE, SIZE), 1)
    return (place(row) == col).astype(F32).astype(BF16)


def device_order(p):
    return (p & 192) + ((p >> 2) & 1) * 32 + ((p >> 3) & 7) * 4 + (p & 3)


def arrival_order(o):
    return ((o >> 2) & 3) * 64 + ((o >> 4) & 1) * 32 + (o & 3) * 8 + (o >> 5)


def gelu_parts(v):
    c = 0.7978845608028654
    th = jnp.tanh(c * (v + 0.044715 * (v * v * v)))
    return c, th


def gelu(v):
    _, th = gelu_parts(v)
    return 0.5 * v * (1.0 + th)


def gelu_slope(v):
    c, th = gelu_parts(v)
    return 0.5 * (1.0 + th) + 0.5 * v * (1.0 - th * th) * (c * (1.0 + 3.0 * 0.044715 * (v * v)))


def block_of(q, h):
    return (q // 8) * 16 + h * 8 + q % 8


def kernel(
    feat, cot, l1, r1, l2, r2,
    in_grad, g_l1, g_r1, g_l2, g_r2,
    perm, turn, eye,
    l1p, r1p, r1tp, l2p, l2t, r2tp, other,
    xs, xr, ps, pr,
    b1, dyk, hid, act, b2, da2, dwk, da1, back,
    part, part1, ring_s, ring_r, line_s, line_r,
    xs_sem, xr_sem, ps_sem, pr_sem, back_sem,
    gs_sem, gr_sem, rs_sem, rr_sem, ls_sem, lr_sem,
):
    zl = lax.axis_index("dp")
    blk = lax.axis_index("block")
    h = (blk // 8) % 2
    q = (blk // 16) * 8 + blk % 8
    z = h * 8 + zl
    scale = float(2048) ** (-0.5)

    def column(zz):
        return (zz % 8, block_of(q, zz // 8))

    up = column((z + 1) % 16)
    down = column((z + 15) % 16)
    across = (zl, block_of(q, 1 - h))

    barrier = pltpu.get_barrier_semaphore()

    def greet(i, carry):
        pl.semaphore_signal(barrier, inc=1, device_id=(zl, (blk + i) % 64), device_id_type=MESH)
        return carry

    lax.fori_loop(1, 64, greet, 0)
    pl.semaphore_signal(barrier, inc=1, device_id=up, device_id_type=MESH)
    pl.semaphore_signal(barrier, inc=1, device_id=down, device_id_type=MESH)
    pl.semaphore_wait(barrier, 65)

    factors = (r1, l2, r2)

    def gather_copy(way, k, src):
        return pltpu.make_async_remote_copy(
            src_ref=src,
            dst_ref=other.at[way, k],
            send_sem=gs_sem.at[way, k],
            recv_sem=gr_sem.at[way, k],
            device_id=up if way == 0 else down,
            device_id_type=MESH,
        )

    def gather_step(s):
        for way in range(2):
            place = zl if way == 0 else 7 - zl
            if s < 12:

                @pl.when(place == 7)
                def _():
                    own_half = factors[s // 4].at[2 * way + (s // 2) % 2, pl.ds((s % 2) * 128, 128)]
                    gather_copy(way, s, own_half).start()

            k = s - 1 - place

            @pl.when(jnp.logical_and(k >= 0, k < 12))
            def _():
                copy = gather_copy(way, k, other.at[way, k])
                copy.wait_recv()

                @pl.when(place < 7)
                def _():
                    copy.start()

    perm[...] = selection(device_order)
    turn[...] = selection(arrival_order)
    eye[...] = selection(lambda r: r)

    for jj in range(4):
        l1p[jj] = dot(perm[...], l1[jj], NN).astype(BF16)

    def cross_pack(n, left, rows):
        for pair in range(2):
            out = [
                dot(left(2 * pair + e), rows[:, pl.ds((2 * pair + e) * SIZE, SIZE)], NT)
                for e in range(2)
            ]
            for half in range(2):
                both = [o[:, half * TOK:(half + 1) * TOK].reshape(PLANE, 8, TOK) for o in out]
                xs[n, pl.ds(half * PLANE, PLANE), pl.ds(pair * 16, 16), :] = jnp.concatenate(
                    both, axis=1
                ).astype(BF16)

    def cross_launch(n, first, last):
        mine = q * 2 + h

        def send(i, carry):
            to = (blk + i) % 64
            to_h = (to // 8) % 2
            to_q = (to // 16) * 8 + to % 8
            pltpu.make_async_remote_copy(
                src_ref=xs.at[n, to_h * PLANE + to_q],
                dst_ref=xr.at[n, mine],
                send_sem=xs_sem.at[n],
                recv_sem=xr_sem.at[n],
                device_id=(zl, to),
                device_id_type=MESH,
            ).start()
            return carry

        lax.fori_loop(first, last, send, 0)
        if first == 1:
            pltpu.make_async_copy(xs.at[n, h * PLANE + q], xr.at[n, mine], xr_sem.at[n]).start()

    def take(group, g, out):
        rows = dot(turn[...], group, NN).astype(BF16).reshape(8, 2, 16, TOK)
        out[:, g // 2, :, g % 2] = rows

    def cross_take(n, out):
        pltpu.make_async_copy(xr.at[n], xr.at[n], xr_sem.at[n]).wait()

        def one(g, carry):
            take(xr[n, pl.ds(g * 8, 8)].reshape(SIZE, TOK), g, out)
            return carry

        lax.fori_loop(0, 8, one, 0)

    def plane_send(n, term):
        def one(pair, carry):
            both = [term(2 * pair + e).reshape(PLANE, 8, TOK) for e in range(2)]
            ps[n, :, pl.ds(pl.multiple_of(pair * 16, 16), 16), :] = jnp.concatenate(
                both, axis=1
            ).astype(BF16)
            return carry

        lax.fori_loop(0, 4, one, 0)

        def send(i, carry):
            to = (q + i) % PLANE
            pltpu.make_async_remote_copy(
                src_ref=ps.at[n, to],
                dst_ref=pr.at[n, q],
                send_sem=ps_sem.at[n],
                recv_sem=pr_sem.at[n],
                device_id=(zl, block_of(to, h)),
                device_id_type=MESH,
            ).start()
            return carry

        lax.fori_loop(1, PLANE, send, 0)
        pltpu.make_async_copy(ps.at[n, q], pr.at[n, q], pr_sem.at[n]).start()

    def plane_take(n, out):
        pltpu.make_async_copy(pr.at[n], pr.at[n], pr_sem.at[n]).wait()

        def one(g, carry):
            take(pr[n, pl.ds(g * 4, 4)].reshape(SIZE, TOK), g, out)
            return carry

        lax.fori_loop(0, 8, one, 0)

    def block(ref, k):
        return ref[k].reshape(SIZE, TOK)

    def own(n, d):
        return part[n, pl.ds((d // 8) * 4, 4), pl.ds(pl.multiple_of((d % 8) * 32, 32), 32), :]

    def ring_copy(n, way, s):
        return pltpu.make_async_remote_copy(
            src_ref=ring_s.at[n, way, s],
            dst_ref=ring_r.at[n, way, s],
            send_sem=rs_sem.at[n, way, s],
            recv_sem=rr_sem.at[n, way, s],
            device_id=up if way == 0 else down,
            device_id_type=MESH,
        )

    def ring_step(n, s):
        for way in range(2 if s < 7 else 1):
            d = (z + 8 - s) % 16 if way == 0 else (z + 9 + s) % 16
            total = own(n, d)
            if s:
                ring_copy(n, way, s - 1).wait_recv()
                total = total + ring_r[n, way, s - 1].astype(F32)
            ring_s[n, way, s] = total.astype(BF16)
            ring_copy(n, way, s).start()

    def ring_end(n, out):
        ring_copy(n, 0, 7).wait_recv()
        ring_copy(n, 1, 6).wait_recv()
        total = own(n, z) + ring_r[n, 0, 7].astype(F32) + ring_r[n, 1, 6].astype(F32)
        out[...] = total * scale

    def own_factor(f):
        return lambda b: factors[f][b]

    def other_factor(f):
        return lambda b: other[b // 2, pl.ds(f * 4 + (b % 2) * 2, 2)].reshape(SIZE, SIZE)

    def prepare(f, src, base):
        def one(b, carry):
            k = base + b
            m = src(b)
            if f == 0:
                r1p[k] = dot(perm[...], m, NN).astype(BF16)
                r1tp[k] = dot(perm[...], m, NT).astype(BF16)
            elif f == 1:
                l2p[k] = dot(perm[...], m, NN).astype(BF16)
                l2t[k] = dot(eye[...], m, NT).astype(BF16)
            else:
                r2tp[k] = dot(perm[...], m, NT).astype(BF16)
            return carry

        lax.fori_loop(0, 4, one, 0)

    def grad_hidden(k):
        grad = dot(l2t[k], block(da2, k), NN)
        grad = (grad * gelu_slope(block(hid, k).astype(F32))).astype(BF16)
        return dot(perm[...], grad, NN)

    def activate(k, carry):
        act[k] = gelu(hid[k].astype(F32)).astype(BF16)
        return carry

    def partial(n, left, right):
        def one(k, carry):
            part[n, k] = dot(block(left, k), block(right, k), NT)
            return carry

        lax.fori_loop(0, 8, one, 0)

    gather_step(0)
    cross_pack(0, lambda jj: l1p[jj], feat)
    cross_launch(0, 1, 64)
    gather_step(1)
    cross_pack(1, lambda jj: perm[...], cot)
    gather_step(2)
    for f in range(3):
        prepare(f, own_factor(f), h * 4)
    for s in range(3, 12):
        gather_step(s)
        cross_launch(1, 1 + 7 * (s - 3), 8 + 7 * (s - 3))
    prepare(0, other_factor(0), (1 - h) * 4)

    cross_take(0, b1)
    plane_send(0, lambda k: dot(r1p[k], block(b1, k), NN))
    for s in range(12, 16):
        gather_step(s)
    prepare(1, other_factor(1), (1 - h) * 4)
    plane_take(0, hid)
    lax.fori_loop(0, 8, activate, 0)
    plane_send(2, lambda k: dot(l2p[k], block(act, k), NN))
    for s in range(16, 20):
        gather_step(s)
    prepare(2, other_factor(2), (1 - h) * 4)
    plane_take(2, b2)

    cross_take(1, dyk)
    plane_send(1, lambda k: dot(r2tp[k], block(dyk, k), NN))
    partial(2, dyk, b2)
    ring_step(2, 0)
    plane_take(1, da2)
    plane_send(3, grad_hidden)
    ring_step(2, 1)
    partial(1, da2, act)
    ring_step(1, 0)
    plane_take(3, dwk)
    plane_send(4, lambda k: dot(r1tp[k], block(dwk, k), NN))
    ring_step(2, 2)
    ring_step(1, 1)
    partial(0, dwk, b1)
    ring_step(0, 0)
    plane_take(4, da1)
    back_copy = pltpu.make_async_remote_copy(
        src_ref=da1.at[pl.ds((1 - h) * 4, 4)],
        dst_ref=back,
        send_sem=back_sem.at[0],
        recv_sem=back_sem.at[1],
        device_id=across,
        device_id_type=MESH,
    )
    back_copy.start()
    for s in range(3, 8):
        ring_step(2, s)
        ring_step(1, s - 1)
        ring_step(0, s - 2)
    back_copy.wait_recv()

    def home_rows(which):
        return pl.ds(pl.multiple_of(which * TOK, TOK), TOK)

    for jj in range(4):
        mine = block(da1, h * 4 + jj)
        theirs = block(back, jj)
        cols = pl.ds(jj * SIZE, SIZE)
        part1[jj] = dot(mine, feat[home_rows(h), cols], NN) + dot(
            theirs, feat[home_rows(1 - h), cols], NN
        )

    def line_copy(way, s):
        return pltpu.make_async_remote_copy(
            src_ref=line_s.at[way, s],
            dst_ref=line_r.at[way, s],
            send_sem=ls_sem.at[way, s],
            recv_sem=lr_sem.at[way, s],
            device_id=up if way == 0 else down,
            device_id_type=MESH,
        )

    def own1(d):
        return part1[:, pl.ds(pl.multiple_of(d * 32, 32), 32), :]

    for s in range(7):
        for way in range(2):
            at = zl if way == 0 else 7 - zl
            d = 7 - (s - at) if way == 0 else s - at
            d = jnp.clip(d, 0, 7)

            @pl.when(jnp.logical_and(at <= s, at > 0))
            def _():
                if s:
                    line_copy(way, s - 1).wait_recv()
                    line_s[way, s] = (own1(d) + line_r[way, s - 1].astype(F32)).astype(BF16)
                    line_copy(way, s).start()

            @pl.when(at == 0)
            def _():
                line_s[way, s] = own1(d).astype(BF16)
                line_copy(way, s).start()

        if s == 0:
            for jj in range(4):
                cols = pl.ds(jj * SIZE, SIZE)
                in_grad[home_rows(h), cols] = dot(block(da1, h * 4 + jj), l1[jj], TN).astype(BF16)
                in_grad[home_rows(1 - h), cols] = dot(block(back, jj), l1[jj], TN).astype(BF16)
        if s == 1:
            ring_end(2, g_r2)
            ring_step(1, 7)
            ring_step(0, 6)
        if s == 3:
            ring_end(1, g_l2)
            ring_step(0, 7)
        if s == 5:
            ring_end(0, g_r1)

    g_l1[...] = own1(zl)
    for way in range(2):
        at = zl if way == 0 else 7 - zl

        @pl.when(at > 0)
        def _():
            line_copy(way, 6).wait_recv()
            g_l1[...] += line_r[way, 6].astype(F32)

    g_l1[...] = g_l1[...] * scale

    for n in range(2):
        sent = xs.at[n, pl.ds(0, 63)]
        pltpu.make_async_copy(sent, sent, xs_sem.at[n]).wait()
    for n in range(5):
        sent = ps.at[n, pl.ds(0, PLANE - 1)]
        pltpu.make_async_copy(sent, sent, ps_sem.at[n]).wait()
    back_copy.wait_send()
    for way in range(2):
        for k in range(12):
            gather_copy(way, k, other.at[way, k]).wait_send()
    for n in range(3):
        for s in range(8):
            ring_copy(n, 0, s).wait_send()
            if s < 7:
                ring_copy(n, 1, s).wait_send()
    for way in range(2):
        at = zl if way == 0 else 7 - zl
        for s in range(7):

            @pl.when(at <= s)
            def _():
                line_copy(way, s).wait_send()


def per_device(features_in, cotangent, left_one, right_one, left_two, right_two):
    vmem = pl.BlockSpec(memory_space=pltpu.VMEM)
    dma = pltpu.SemaphoreType.DMA
    square = (SIZE, SIZE)
    grad = jax.ShapeDtypeStruct((4, 32, SIZE), F32)
    arrived = pltpu.VMEM((8, 4, 2, 2, 16, TOK), BF16)
    eight = pltpu.VMEM((8,) + square, BF16)
    outs = pl.pallas_call(
        kernel,
        name="monarch",
        out_shape=(jax.ShapeDtypeStruct(features_in.shape, BF16), grad, grad, grad, grad),
        in_specs=[vmem] * 6,
        out_specs=(vmem,) * 5,
        scratch_shapes=[
            pltpu.VMEM(square, BF16),
            pltpu.VMEM(square, BF16),
            pltpu.VMEM(square, BF16),
            pltpu.VMEM((4,) + square, BF16),
            eight, eight, eight, eight, eight,
            pltpu.VMEM((2, 12, 128, SIZE), BF16),
            pltpu.VMEM((2, 64, 32, TOK), BF16),
            pltpu.VMEM((2, 64, 32, TOK), BF16),
            pltpu.VMEM((5, PLANE, 64, TOK), BF16),
            pltpu.VMEM((5, PLANE, 64, TOK), BF16),
            arrived, arrived, arrived, arrived, arrived, arrived, arrived, arrived,
            pltpu.VMEM((4, 4, 2, 2, 16, TOK), BF16),
            pltpu.VMEM((3, 8) + square, F32),
            pltpu.VMEM((4,) + square, F32),
            pltpu.VMEM((3, 2, 8, 4, 32, SIZE), BF16),
            pltpu.VMEM((3, 2, 8, 4, 32, SIZE), BF16),
            pltpu.VMEM((2, 7, 4, 32, SIZE), BF16),
            pltpu.VMEM((2, 7, 4, 32, SIZE), BF16),
            dma((2,)), dma((2,)), dma((5,)), dma((5,)), dma((2,)),
            dma((2, 12)), dma((2, 12)), dma((3, 2, 8)), dma((3, 2, 8)), dma((2, 7)), dma((2, 7)),
        ],
        compiler_params=pltpu.CompilerParams(
            collective_id=0, has_side_effects=True, vmem_limit_bytes=56 << 20
        ),
        cost_estimate=pl.CostEstimate(
            flops=4_000_000_000, bytes_accessed=5_000_000, transcendentals=600_000
        ),
    )(features_in, cotangent, left_one, right_one, left_two, right_two)
    return (outs[0],) + tuple(jnp.swapaxes(g, 0, 1) for g in outs[1:])


def solution(mesh):
    return jax.shard_map(
        per_device,
        mesh=mesh,
        in_specs=(
            P("dp", "block"),
            P("dp", "block"),
            P("block", None, None),
            P("block", None, None),
            P("block", None, None),
            P("block", None, None),
        ),
        out_specs=(
            P("dp", "block"),
            P("dp", "block", None),
            P("dp", "block", None),
            P("dp", "block", None),
            P("dp", "block", None),
        ),
        check_vma=False,
    )
```

time: 451 us -> 240 us (0.53)
  waiting for transfers between devices: 298 us -> 0 us
  Pallas kernels: 0 us -> 231 us
  starting transfers between devices: 98.4 us -> 0 us
  local copies, waits for them, and re-layouts: 23.4 us -> 5.8 us
  between operations: 15 us -> 0.66 us
  matrix products: 11.4 us -> 0 us
    pallas_call x0 -> x1, Pallas kernels: none -> 231 us  [per_device(): pl.pallas_call(kernel, name='monarch', out_shape=(jax.ShapeDtypeStruct(fe...]
    all_to_all x7 -> x0, waiting for transfers between devices: 122 us -> none  [the longest x1 25.2 us: per_device(): lax.all_to_all(turned(second_out), 'block', split_axis=1, concat_axis=2,...]
    unnamed x3 -> x0, waiting for transfers between devices: 118 us -> none
    all_to_all x7 -> x0, starting transfers between devices: 98.3 us -> none  [the longest x1 22.2 us: per_device(): lax.all_to_all(turned(second_out), 'block', split_axis=1, concat_axis=2,...]
    reduce_scatter x1 -> x0, waiting for transfers between devices: 58.7 us -> none  [per_device(): lax.psum_scatter(terms[3].astype(jnp.bfloat16), 'dp', scatter_dimension=0...]
    dot_general x11 -> x0, matrix products: 11.4 us -> none  [the longest x4 3.47 us: compute(): jnp.einsum(form, cot_part, act_part, preferred_element_type=jnp.float32)]
    convert_element_type x10 -> x0, local copies, waits for them, and re-layouts: 10.4 us -> none  [the longest x2 1.66 us: per_device(): hidden32 = hidden.astype(f32)]
    all_to_all x10 -> x0, local copies, waits for them, and re-layouts: 5.5 us -> none  [the longest x2 1.57 us: per_device(): lax.all_to_all(turned(back_two), 'block', split_axis=1, concat_axis=2, ti...]
  transfers between devices with their start and end apart: 9 -> 0, of which waited for: 9 -> 0; matrix products, arithmetic and copies ran while one was open for 6% -> 0% of each run, Pallas kernels for 0% -> 0%
where the time goes in v1:
time: 240 us; the launch traced here: 237 us
  Pallas kernels  231 us (96%)
  local copies, waits for them, and re-layouts  5.8 us (2%)
    pallas_call x1, Pallas kernels, per_device(): pl.pallas_call(kernel, name='monarch', out_shape=(jax.ShapeDtypeStruct(fe...  231 us
    unnamed x11, local copies, waits for them, and re-layouts  5.8 us

profile of v1, /device:TPU:6, one launch (start us, length us, event | category | flops | bytes accessed | tf_op | source)
XLA Modules:
  0.0 237.4 jit_solution(5346194461147571332)
XLA Ops:
  0.6 230.9 %monarch.1 = (bf16[256,1024]{1,0:T(8,128)(2,1)}, f32[4,32,256]{2,1,0:T(8,128)}, f32[4,32,256]{2,1,0:T(8,128)}, f32[4,32,256]{2,1,0:T(8,128)}, f32[4,32,256]{2,1,0:T(8,128)}) custom-call(bf16[256,1024]{1,0:T(8,128)(2,1)} %feat.1, bf16[256,1024]{1,0:T(8,128)(2,1)} %cot.1, bf16[4,256,256]{2,1,0:T(8,128)(2,1)} %l1.1, bf16[4,256,256]{2,1,0:T(8,128)(2,1)} %r1.1, ...), custom_call_target="tpu_custom_call" | custom-call | flops 4000000000 | bytes 5000000 | tf_op jit(solution)/shard_map/monarch/pallas_call | solution.py:439
  231.6 0.0 copy-start.2
  231.6 0.0 copy-start
  231.6 1.7 copy.11
  233.3 1.6 copy.12
  234.9 0.0 copy-done.2
  234.9 0.0 copy-start.1
  235.0 0.7 copy.13
  235.7 0.2 copy-done.1
  235.9 0.7 copy.14
  236.6 0.0 copy-done
  236.6 0.8 copy.16
Async XLA Ops:
  231.6 3.4 %copy-start.2 = (f32[4,32,256]{2,1,0:T(8,128)S(1)}, f32[4,32,256]{2,1,0:T(8,128)}, u32[]{:S(2)}) copy-start(f32[4,32,256]{2,1,0:T(8,128)} %get-tuple-element.13) | copy-start | bytes 393220
  231.6 5.0 %copy-start = (bf16[256,1024]{1,0:T(8,128)(2,1)S(1)}, bf16[256,1024]{1,0:T(8,128)(2,1)}, u32[]{:S(2)}) copy-start(bf16[256,1024]{1,0:T(8,128)(2,1)} %get-tuple-element.25) | copy-start | bytes 1572868
  234.9 0.9 copy-start.1

commit v2 on v1

--- a/solution.py
+++ b/solution.py
@@ -51,7 +51,7 @@
 
 
 def block_of(q, h):
-    return (q // 8) * 16 + h * 8 + q % 8
+    return ((q >> 3) << 4) + (h << 3) + (q & 7)
 
 
 def kernel(
@@ -61,7 +61,7 @@
     l1p, r1p, r1tp, l2p, l2t, r2tp, other,
     xs, xr, ps, pr,
     b1, dyk, hid, act, b2, da2, dwk, da1, back,
-    part, part1, ring_s, ring_r, line_s, line_r,
+    part, part1, last, ring_s, ring_r, line_s, line_r,
     xs_sem, xr_sem, ps_sem, pr_sem, back_sem,
     gs_sem, gr_sem, rs_sem, rr_sem, ls_sem, lr_sem,
 ):
@@ -82,13 +82,12 @@
     barrier = pltpu.get_barrier_semaphore()
 
     def greet(i, carry):
-        pl.semaphore_signal(barrier, inc=1, device_id=(zl, (blk + i) % 64), device_id_type=MESH)
+        pl.semaphore_signal(barrier, inc=1, device_id=(zl, (blk + i) & 63), device_id_type=MESH)
         return carry
 
     lax.fori_loop(1, 64, greet, 0)
     pl.semaphore_signal(barrier, inc=1, device_id=up, device_id_type=MESH)
     pl.semaphore_signal(barrier, inc=1, device_id=down, device_id_type=MESH)
-    pl.semaphore_wait(barrier, 65)
 
     factors = (r1, l2, r2)
 
@@ -102,26 +101,36 @@
             device_id_type=MESH,
         )
 
-    def gather_step(s):
+    def gather_source(f):
         for way in range(2):
             place = zl if way == 0 else 7 - zl
-            if s < 12:
-
-                @pl.when(place == 7)
+
+            @pl.when(place == 7)
+            def _():
+                for k in range(8):
+                    own_half = factors[f].at[2 * way + k // 4, pl.ds((k % 4) * 64, 64)]
+                    gather_copy(way, f * 8 + k, own_half).start()
+
+    def gather_run(first, last, also=None):
+        def one(when, carry):
+            for way in range(2):
+                place = zl if way == 0 else 7 - zl
+                k = when - 3 * place
+
+                @pl.when(jnp.logical_and(k >= 0, k < 24))
                 def _():
-                    own_half = factors[s // 4].at[2 * way + (s // 2) % 2, pl.ds((s % 2) * 128, 128)]
-                    gather_copy(way, s, own_half).start()
-
-            k = s - 1 - place
-
-            @pl.when(jnp.logical_and(k >= 0, k < 12))
-            def _():
-                copy = gather_copy(way, k, other.at[way, k])
-                copy.wait_recv()
-
-                @pl.when(place < 7)
-                def _():
-                    copy.start()
+                    copy = gather_copy(way, k, other.at[way, k])
+                    copy.wait_recv()
+
+                    @pl.when(place < 7)
+                    def _():
+                        copy.start()
+
+            if also is not None:
+                also(when)
+            return carry
+
+        lax.fori_loop(first, last, one, 0)
 
     perm[...] = selection(device_order)
     turn[...] = selection(arrival_order)
@@ -146,9 +155,9 @@
         mine = q * 2 + h
 
         def send(i, carry):
-            to = (blk + i) % 64
-            to_h = (to // 8) % 2
-            to_q = (to // 16) * 8 + to % 8
+            to = (blk + i) & 63
+            to_h = (to >> 3) & 1
+            to_q = ((to >> 4) << 3) + (to & 7)
             pltpu.make_async_remote_copy(
                 src_ref=xs.at[n, to_h * PLANE + to_q],
                 dst_ref=xr.at[n, mine],
@@ -160,21 +169,26 @@
             return carry
 
         lax.fori_loop(first, last, send, 0)
-        if first == 1:
-            pltpu.make_async_copy(xs.at[n, h * PLANE + q], xr.at[n, mine], xr_sem.at[n]).start()
-
-    def take(group, g, out):
-        rows = dot(turn[...], group, NN).astype(BF16).reshape(8, 2, 16, TOK)
-        out[:, g // 2, :, g % 2] = rows
+
+    def cross_own(n):
+        pltpu.make_async_copy(
+            xs.at[n, h * PLANE + q], xr.at[n, q * 2 + h], xr_sem.at[n]
+        ).start()
+
+    def take(groups, pair, out):
+        rows = dot(turn[...], jnp.concatenate(groups, axis=1), NN).astype(BF16)
+        for e in range(2):
+            out[:, pair, :, e] = rows[:, e * TOK:(e + 1) * TOK].reshape(8, 2, 16, TOK)
 
     def cross_take(n, out):
         pltpu.make_async_copy(xr.at[n], xr.at[n], xr_sem.at[n]).wait()
 
-        def one(g, carry):
-            take(xr[n, pl.ds(g * 8, 8)].reshape(SIZE, TOK), g, out)
-            return carry
-
-        lax.fori_loop(0, 8, one, 0)
+        def one(pair, carry):
+            groups = [xr[n, pl.ds(pair * 16 + e * 8, 8)].reshape(SIZE, TOK) for e in range(2)]
+            take(groups, pair, out)
+            return carry
+
+        lax.fori_loop(0, 4, one, 0, unroll=True)
 
     def plane_send(n, term):
         def one(pair, carry):
@@ -184,10 +198,10 @@
             ).astype(BF16)
             return carry
 
-        lax.fori_loop(0, 4, one, 0)
+        lax.fori_loop(0, 4, one, 0, unroll=True)
 
         def send(i, carry):
-            to = (q + i) % PLANE
+            to = (q + i) & (PLANE - 1)
             pltpu.make_async_remote_copy(
                 src_ref=ps.at[n, to],
                 dst_ref=pr.at[n, q],
@@ -204,11 +218,12 @@
     def plane_take(n, out):
         pltpu.make_async_copy(pr.at[n], pr.at[n], pr_sem.at[n]).wait()
 
-        def one(g, carry):
-            take(pr[n, pl.ds(g * 4, 4)].reshape(SIZE, TOK), g, out)
-            return carry
-
-        lax.fori_loop(0, 8, one, 0)
+        def one(pair, carry):
+            groups = [pr[n, pl.ds(pair * 8 + e * 4, 4)].reshape(SIZE, TOK) for e in range(2)]
+            take(groups, pair, out)
+            return carry
+
+        lax.fori_loop(0, 4, one, 0, unroll=True)
 
     def block(ref, k):
         return ref[k].reshape(SIZE, TOK)
@@ -240,13 +255,14 @@
         ring_copy(n, 0, 7).wait_recv()
         ring_copy(n, 1, 6).wait_recv()
         total = own(n, z) + ring_r[n, 0, 7].astype(F32) + ring_r[n, 1, 6].astype(F32)
-        out[...] = total * scale
+        for j in range(4):
+            out[:, j, :] = total[j] * scale
 
     def own_factor(f):
         return lambda b: factors[f][b]
 
     def other_factor(f):
-        return lambda b: other[b // 2, pl.ds(f * 4 + (b % 2) * 2, 2)].reshape(SIZE, SIZE)
+        return lambda b: other[b // 2, pl.ds(f * 8 + (b % 2) * 4, 4)].reshape(SIZE, SIZE)
 
     def prepare(f, src, base):
         def one(b, carry):
@@ -262,7 +278,7 @@
                 r2tp[k] = dot(perm[...], m, NT).astype(BF16)
             return carry
 
-        lax.fori_loop(0, 4, one, 0)
+        lax.fori_loop(0, 4, one, 0, unroll=True)
 
     def grad_hidden(k):
         grad = dot(l2t[k], block(da2, k), NN)
@@ -278,31 +294,37 @@
             part[n, k] = dot(block(left, k), block(right, k), NT)
             return carry
 
-        lax.fori_loop(0, 8, one, 0)
-
-    gather_step(0)
+        lax.fori_loop(0, 8, one, 0, unroll=True)
+
     cross_pack(0, lambda jj: l1p[jj], feat)
-    cross_launch(0, 1, 64)
-    gather_step(1)
+    pl.semaphore_wait(barrier, 65)
+    gather_source(0)
+    cross_own(0)
+    gather_source(1)
     cross_pack(1, lambda jj: perm[...], cot)
-    gather_step(2)
+    cross_own(1)
+    gather_source(2)
     for f in range(3):
         prepare(f, own_factor(f), h * 4)
-    for s in range(3, 12):
-        gather_step(s)
-        cross_launch(1, 1 + 7 * (s - 3), 8 + 7 * (s - 3))
+    def pace(when):
+        cross_launch(0, jnp.minimum(3 * when + 1, 64), jnp.minimum(3 * when + 4, 64))
+        late = jnp.maximum(when - 22, 0)
+        cross_launch(
+            1, jnp.minimum(3 * late + 1, 64),
+            jnp.where(when < 22, 1, jnp.minimum(3 * late + 4, 64)),
+        )
+
+    gather_run(0, 29, pace)
     prepare(0, other_factor(0), (1 - h) * 4)
 
     cross_take(0, b1)
     plane_send(0, lambda k: dot(r1p[k], block(b1, k), NN))
-    for s in range(12, 16):
-        gather_step(s)
+    gather_run(29, 37, pace)
     prepare(1, other_factor(1), (1 - h) * 4)
     plane_take(0, hid)
-    lax.fori_loop(0, 8, activate, 0)
+    lax.fori_loop(0, 8, activate, 0, unroll=True)
     plane_send(2, lambda k: dot(l2p[k], block(act, k), NN))
-    for s in range(16, 20):
-        gather_step(s)
+    gather_run(37, 45, pace)
     prepare(2, other_factor(2), (1 - h) * 4)
     plane_take(2, b2)
 
@@ -310,43 +332,57 @@
     plane_send(1, lambda k: dot(r2tp[k], block(dyk, k), NN))
     partial(2, dyk, b2)
     ring_step(2, 0)
+    ring_step(2, 1)
     plane_take(1, da2)
     plane_send(3, grad_hidden)
-    ring_step(2, 1)
+    ring_step(2, 2)
     partial(1, da2, act)
     ring_step(1, 0)
+    ring_step(2, 3)
+    ring_step(1, 1)
     plane_take(3, dwk)
     plane_send(4, lambda k: dot(r1tp[k], block(dwk, k), NN))
-    ring_step(2, 2)
-    ring_step(1, 1)
+    ring_step(2, 4)
+    ring_step(1, 2)
     partial(0, dwk, b1)
     ring_step(0, 0)
+    ring_step(2, 5)
+    ring_step(1, 3)
+    ring_step(0, 1)
     plane_take(4, da1)
-    back_copy = pltpu.make_async_remote_copy(
-        src_ref=da1.at[pl.ds((1 - h) * 4, 4)],
-        dst_ref=back,
-        send_sem=back_sem.at[0],
-        recv_sem=back_sem.at[1],
-        device_id=across,
-        device_id_type=MESH,
-    )
-    back_copy.start()
-    for s in range(3, 8):
-        ring_step(2, s)
-        ring_step(1, s - 1)
-        ring_step(0, s - 2)
-    back_copy.wait_recv()
+    def back_copy(c):
+        return pltpu.make_async_remote_copy(
+            src_ref=da1.at[pl.ds((1 - h) * 4, 4), c // 2, c % 2],
+            dst_ref=back.at[pl.ds(0, 4), c // 2, c % 2],
+            send_sem=back_sem.at[0, c],
+            recv_sem=back_sem.at[1, c],
+            device_id=across,
+            device_id_type=MESH,
+        )
+
+    for c in (7, 0, 6, 1, 5, 2, 4, 3):
+        back_copy(c).start()
 
     def home_rows(which):
         return pl.ds(pl.multiple_of(which * TOK, TOK), TOK)
 
     for jj in range(4):
         mine = block(da1, h * 4 + jj)
-        theirs = block(back, jj)
-        cols = pl.ds(jj * SIZE, SIZE)
-        part1[jj] = dot(mine, feat[home_rows(h), cols], NN) + dot(
-            theirs, feat[home_rows(1 - h), cols], NN
-        )
+        part1[jj] = dot(mine, feat[home_rows(h), pl.ds(jj * SIZE, SIZE)], NN)
+
+    def home_part(c):
+        back_copy(c).wait_recv()
+        for jj in range(4):
+            theirs = back[jj, c // 2, c % 2].reshape(32, TOK)
+            part1[jj, pl.ds(c * 32, 32)] += dot(
+                theirs, feat[home_rows(1 - h), pl.ds(jj * SIZE, SIZE)], NN
+            )
+
+    def ring_steps(*steps):
+        for n, s in steps:
+            ring_step(n, s)
+
+    ring_steps((2, 6), (1, 4), (0, 2))
 
     def line_copy(way, s):
         return pltpu.make_async_remote_copy(
@@ -362,6 +398,9 @@
         return part1[:, pl.ds(pl.multiple_of(d * 32, 32), 32), :]
 
     for s in range(7):
+        if s < 4:
+            home_part(7 - s)
+            home_part(s)
         for way in range(2):
             at = zl if way == 0 else 7 - zl
             d = 7 - (s - at) if way == 0 else s - at
@@ -380,30 +419,35 @@
                 line_copy(way, s).start()
 
         if s == 0:
+            ring_steps((2, 7), (1, 5), (0, 3))
+        if s == 1:
+            ring_end(2, g_r2)
+            ring_steps((1, 6), (0, 4))
+        if s == 2:
+            ring_steps((1, 7), (0, 5))
+        if s == 3:
+            ring_end(1, g_l2)
+            ring_step(0, 6)
+        if s == 4:
             for jj in range(4):
                 cols = pl.ds(jj * SIZE, SIZE)
                 in_grad[home_rows(h), cols] = dot(block(da1, h * 4 + jj), l1[jj], TN).astype(BF16)
                 in_grad[home_rows(1 - h), cols] = dot(block(back, jj), l1[jj], TN).astype(BF16)
-        if s == 1:
-            ring_end(2, g_r2)
-            ring_step(1, 7)
-            ring_step(0, 6)
-        if s == 3:
-            ring_end(1, g_l2)
             ring_step(0, 7)
-        if s == 5:
+        if s == 6:
             ring_end(0, g_r1)
 
-    g_l1[...] = own1(zl)
+    last[...] = own1(zl)
     for way in range(2):
         at = zl if way == 0 else 7 - zl
 
         @pl.when(at > 0)
         def _():
             line_copy(way, 6).wait_recv()
-            g_l1[...] += line_r[way, 6].astype(F32)
-
-    g_l1[...] = g_l1[...] * scale
+            last[...] += line_r[way, 6].astype(F32)
+
+    for j in range(4):
+        g_l1[:, j, :] = last[j] * scale
 
     for n in range(2):
         sent = xs.at[n, pl.ds(0, 63)]
@@ -411,9 +455,10 @@
     for n in range(5):
         sent = ps.at[n, pl.ds(0, PLANE - 1)]
         pltpu.make_async_copy(sent, sent, ps_sem.at[n]).wait()
-    back_copy.wait_send()
+    for c in range(8):
+        back_copy(c).wait_send()
     for way in range(2):
-        for k in range(12):
+        for k in range(24):
             gather_copy(way, k, other.at[way, k]).wait_send()
     for n in range(3):
         for s in range(8):
@@ -433,7 +478,7 @@
     vmem = pl.BlockSpec(memory_space=pltpu.VMEM)
     dma = pltpu.SemaphoreType.DMA
     square = (SIZE, SIZE)
-    grad = jax.ShapeDtypeStruct((4, 32, SIZE), F32)
+    grad = jax.ShapeDtypeStruct((32, 4, SIZE), F32)
     arrived = pltpu.VMEM((8, 4, 2, 2, 16, TOK), BF16)
     eight = pltpu.VMEM((8,) + square, BF16)
     outs = pl.pallas_call(
@@ -448,7 +493,7 @@
             pltpu.VMEM(square, BF16),
             pltpu.VMEM((4,) + square, BF16),
             eight, eight, eight, eight, eight,
-            pltpu.VMEM((2, 12, 128, SIZE), BF16),
+            pltpu.VMEM((2, 24, 64, SIZE), BF16),
             pltpu.VMEM((2, 64, 32, TOK), BF16),
             pltpu.VMEM((2, 64, 32, TOK), BF16),
             pltpu.VMEM((5, PLANE, 64, TOK), BF16),
@@ -457,12 +502,13 @@
             pltpu.VMEM((4, 4, 2, 2, 16, TOK), BF16),
             pltpu.VMEM((3, 8) + square, F32),
             pltpu.VMEM((4,) + square, F32),
+            pltpu.VMEM((4, 32, SIZE), F32),
             pltpu.VMEM((3, 2, 8, 4, 32, SIZE), BF16),
             pltpu.VMEM((3, 2, 8, 4, 32, SIZE), BF16),
             pltpu.VMEM((2, 7, 4, 32, SIZE), BF16),
             pltpu.VMEM((2, 7, 4, 32, SIZE), BF16),
-            dma((2,)), dma((2,)), dma((5,)), dma((5,)), dma((2,)),
-            dma((2, 12)), dma((2, 12)), dma((3, 2, 8)), dma((3, 2, 8)), dma((2, 7)), dma((2, 7)),
+            dma((2,)), dma((2,)), dma((5,)), dma((5,)), dma((2, 8)),
+            dma((2, 24)), dma((2, 24)), dma((3, 2, 8)), dma((3, 2, 8)), dma((2, 7)), dma((2, 7)),
         ],
         compiler_params=pltpu.CompilerParams(
             collective_id=0, has_side_effects=True, vmem_limit_bytes=56 << 20
@@ -471,7 +517,7 @@
             flops=4_000_000_000, bytes_accessed=5_000_000, transcendentals=600_000
         ),
     )(features_in, cotangent, left_one, right_one, left_two, right_two)
-    return (outs[0],) + tuple(jnp.swapaxes(g, 0, 1) for g in outs[1:])
+    return outs
 
 
 def solution(mesh):

time: 240 us -> 201 us (0.84)
  Pallas kernels: 231 us -> 193 us
    pallas_call x1, Pallas kernels: 231 us -> 193 us  [per_device(): pl.pallas_call(kernel, name='monarch', out_shape=(jax.ShapeDtypeStruct(fe...]
    unnamed x11 -> x13, local copies, waits for them, and re-layouts: 5.8 us -> 5.41 us
where the time goes in v2:
time: 201 us; the launch traced here: 199 us
  Pallas kernels  193 us (96%)
  local copies, waits for them, and re-layouts  5.41 us (3%)
    pallas_call x1, Pallas kernels, per_device(): pl.pallas_call(kernel, name='monarch', out_shape=(jax.ShapeDtypeStruct(fe...  193 us
    unnamed x13, local copies, waits for them, and re-layouts  5.41 us

profile of v2, /device:TPU:6, one launch (start us, length us, event | category | flops | bytes accessed | tf_op | source)
XLA Modules:
  0.0 198.9 jit_solution(7263245611863779417)
XLA Ops:
  0.6 192.8 %monarch.1 = (bf16[256,1024]{1,0:T(8,128)(2,1)}, f32[32,4,256]{2,1,0:T(4,128)}, f32[32,4,256]{2,1,0:T(4,128)}, f32[32,4,256]{2,1,0:T(4,128)}, f32[32,4,256]{2,1,0:T(4,128)}) custom-call(bf16[256,1024]{1,0:T(8,128)(2,1)} %feat.1, bf16[256,1024]{1,0:T(8,128)(2,1)} %cot.1, bf16[4,256,256]{2,1,0:T(8,128)(2,1)} %l1.1, bf16[4,256,256]{2,1,0:T(8,128)(2,1)} %r1.1, ...), custom_call_target="tpu_custom_call" | custom-call | flops 4000000000 | bytes 5000000 | tf_op jit(solution)/shard_map/monarch/pallas_call | solution.py:484
  193.5 0.0 copy-start.3
  193.5 1.9 copy.16
  195.4 0.0 copy-done.3
  195.4 0.0 copy-start.2
  195.4 0.7 copy.17
  196.0 0.3 copy-done.2
  196.3 0.0 copy-start.1
  196.3 0.7 copy.18
  197.0 0.3 copy-done.1
  197.3 0.0 copy-start
  197.3 0.7 copy.19
  197.9 0.3 copy-done
  198.2 0.7 copy.20
Async XLA Ops:
  193.5 1.9 copy-start.3
  195.4 1.0 copy-start.2
  196.3 1.0 copy-start.1
  197.3 1.0 copy-start

commit v3 on v2

--- a/solution.py
+++ b/solution.py
@@ -11,6 +11,10 @@
 SIZE = 256
 TOK = 128
 PLANE = 32
+PARTNERS = sorted(
+    ((dx, dy, dc) for dx in range(4) for dy in range(4) for dc in range(2) if (dx, dy, dc) != (0, 0, 0)),
+    key=lambda o: -(min(o[0], 4 - o[0]) + min(o[1], 4 - o[1])),
+)
 NN = ((1,), (0,))
 NT = ((1,), (1,))
 TN = ((0,), (0,))
@@ -55,12 +59,13 @@
 
 
 def kernel(
-    feat, cot, l1, r1, l2, r2,
+    feat_in, cot_in, l1_in, r1_in, l2_in, r2_in,
     in_grad, g_l1, g_r1, g_l2, g_r2,
+    feat, cot, l1, r1, l2, r2, load_sem,
     perm, turn, eye,
     l1p, r1p, r1tp, l2p, l2t, r2tp, other,
     xs, xr, ps, pr,
-    b1, dyk, hid, act, b2, da2, dwk, da1, back,
+    b1, dyk, hid, slope, act, b2, da2, dwk, da1, back,
     part, part1, last, ring_s, ring_r, line_s, line_r,
     xs_sem, xr_sem, ps_sem, pr_sem, back_sem,
     gs_sem, gr_sem, rs_sem, rr_sem, ls_sem, lr_sem,
@@ -79,6 +84,15 @@
     down = column((z + 15) % 16)
     across = (zl, block_of(q, 1 - h))
 
+    loads = [
+        pltpu.make_async_copy(src, dst, load_sem.at[i])
+        for i, (src, dst) in enumerate(
+            ((feat_in, feat), (l1_in, l1), (r1_in, r1), (cot_in, cot), (l2_in, l2), (r2_in, r2))
+        )
+    ]
+    for load in loads:
+        load.start()
+
     barrier = pltpu.get_barrier_semaphore()
 
     def greet(i, carry):
@@ -136,6 +150,8 @@
     turn[...] = selection(arrival_order)
     eye[...] = selection(lambda r: r)
 
+    loads[0].wait()
+    loads[1].wait()
     for jj in range(4):
         l1p[jj] = dot(perm[...], l1[jj], NN).astype(BF16)
 
@@ -200,8 +216,8 @@
 
         lax.fori_loop(0, 4, one, 0, unroll=True)
 
-        def send(i, carry):
-            to = (q + i) & (PLANE - 1)
+        for dx, dy, dc in PARTNERS:
+            to = (((q >> 3) + dx) & 3) * 8 + (((q >> 1) + dy) & 3) * 2 + ((q + dc) & 1)
             pltpu.make_async_remote_copy(
                 src_ref=ps.at[n, to],
                 dst_ref=pr.at[n, q],
@@ -210,9 +226,6 @@
                 device_id=(zl, block_of(to, h)),
                 device_id_type=MESH,
             ).start()
-            return carry
-
-        lax.fori_loop(1, PLANE, send, 0)
         pltpu.make_async_copy(ps.at[n, q], pr.at[n, q], pr_sem.at[n]).start()
 
     def plane_take(n, out):
@@ -282,13 +295,17 @@
 
     def grad_hidden(k):
         grad = dot(l2t[k], block(da2, k), NN)
-        grad = (grad * gelu_slope(block(hid, k).astype(F32))).astype(BF16)
+        grad = (grad * block(slope, k)).astype(BF16)
         return dot(perm[...], grad, NN)
 
     def activate(k, carry):
         act[k] = gelu(hid[k].astype(F32)).astype(BF16)
         return carry
 
+    def derive(k, carry):
+        slope[k] = gelu_slope(hid[k].astype(F32))
+        return carry
+
     def partial(n, left, right):
         def one(k, carry):
             part[n, k] = dot(block(left, k), block(right, k), NT)
@@ -297,6 +314,8 @@
         lax.fori_loop(0, 8, one, 0, unroll=True)
 
     cross_pack(0, lambda jj: l1p[jj], feat)
+    for load in loads[2:]:
+        load.wait()
     pl.semaphore_wait(barrier, 65)
     gather_source(0)
     cross_own(0)
@@ -327,6 +346,7 @@
     gather_run(37, 45, pace)
     prepare(2, other_factor(2), (1 - h) * 4)
     plane_take(2, b2)
+    lax.fori_loop(0, 8, derive, 0, unroll=True)
 
     cross_take(1, dyk)
     plane_send(1, lambda k: dot(r2tp[k], block(dyk, k), NN))
@@ -384,39 +404,42 @@
 
     ring_steps((2, 6), (1, 4), (0, 2))
 
-    def line_copy(way, s):
+    def line_copy(way, s, e):
         return pltpu.make_async_remote_copy(
-            src_ref=line_s.at[way, s],
-            dst_ref=line_r.at[way, s],
-            send_sem=ls_sem.at[way, s],
-            recv_sem=lr_sem.at[way, s],
+            src_ref=line_s.at[way, s, e],
+            dst_ref=line_r.at[way, s, e],
+            send_sem=ls_sem.at[way, s, e],
+            recv_sem=lr_sem.at[way, s, e],
             device_id=up if way == 0 else down,
             device_id_type=MESH,
         )
 
-    def own1(d):
-        return part1[:, pl.ds(pl.multiple_of(d * 32, 32), 32), :]
+    def own1(d, e):
+        return part1[pl.ds(2 * e, 2), pl.ds(pl.multiple_of(d * 32, 32), 32), :]
 
     for s in range(7):
         if s < 4:
             home_part(7 - s)
             home_part(s)
-        for way in range(2):
-            at = zl if way == 0 else 7 - zl
-            d = 7 - (s - at) if way == 0 else s - at
-            d = jnp.clip(d, 0, 7)
-
-            @pl.when(jnp.logical_and(at <= s, at > 0))
-            def _():
+        for e in range(2):
+            for way in range(2):
+                at = zl if way == 0 else 7 - zl
+                d = 7 - (s - at) if way == 0 else s - at
+                d = jnp.clip(d, 0, 7)
+
                 if s:
-                    line_copy(way, s - 1).wait_recv()
-                    line_s[way, s] = (own1(d) + line_r[way, s - 1].astype(F32)).astype(BF16)
-                    line_copy(way, s).start()
-
-            @pl.when(at == 0)
-            def _():
-                line_s[way, s] = own1(d).astype(BF16)
-                line_copy(way, s).start()
+
+                    @pl.when(jnp.logical_and(at <= s, at > 0))
+                    def _():
+                        line_copy(way, s - 1, e).wait_recv()
+                        total = own1(d, e) + line_r[way, s - 1, e].astype(F32)
+                        line_s[way, s, e] = total.astype(BF16)
+                        line_copy(way, s, e).start()
+
+                @pl.when(at == 0)
+                def _():
+                    line_s[way, s, e] = own1(d, e).astype(BF16)
+                    line_copy(way, s, e).start()
 
         if s == 0:
             ring_steps((2, 7), (1, 5), (0, 3))
@@ -437,17 +460,18 @@
         if s == 6:
             ring_end(0, g_r1)
 
-    last[...] = own1(zl)
-    for way in range(2):
-        at = zl if way == 0 else 7 - zl
-
-        @pl.when(at > 0)
-        def _():
-            line_copy(way, 6).wait_recv()
-            last[...] += line_r[way, 6].astype(F32)
-
-    for j in range(4):
-        g_l1[:, j, :] = last[j] * scale
+    for e in range(2):
+        last[e] = own1(zl, e)
+        for way in range(2):
+            at = zl if way == 0 else 7 - zl
+
+            @pl.when(at > 0)
+            def _():
+                line_copy(way, 6, e).wait_recv()
+                last[e] += line_r[way, 6, e].astype(F32)
+
+        for j in range(2):
+            g_l1[:, 2 * e + j, :] = last[e, j] * scale
 
     for n in range(2):
         sent = xs.at[n, pl.ds(0, 63)]
@@ -471,7 +495,8 @@
 
             @pl.when(at <= s)
             def _():
-                line_copy(way, s).wait_send()
+                line_copy(way, s, 0).wait_send()
+                line_copy(way, s, 1).wait_send()
 
 
 def per_device(features_in, cotangent, left_one, right_one, left_two, right_two):
@@ -485,9 +510,16 @@
         kernel,
         name="monarch",
         out_shape=(jax.ShapeDtypeStruct(features_in.shape, BF16), grad, grad, grad, grad),
-        in_specs=[vmem] * 6,
+        in_specs=[pl.BlockSpec(memory_space=pl.ANY)] * 6,
         out_specs=(vmem,) * 5,
         scratch_shapes=[
+            pltpu.VMEM(features_in.shape, BF16),
+            pltpu.VMEM(features_in.shape, BF16),
+            pltpu.VMEM((4,) + square, BF16),
+            pltpu.VMEM((4,) + square, BF16),
+            pltpu.VMEM((4,) + square, BF16),
+            pltpu.VMEM((4,) + square, BF16),
+            dma((6,)),
             pltpu.VMEM(square, BF16),
             pltpu.VMEM(square, BF16),
             pltpu.VMEM(square, BF16),
@@ -498,17 +530,17 @@
             pltpu.VMEM((2, 64, 32, TOK), BF16),
             pltpu.VMEM((5, PLANE, 64, TOK), BF16),
             pltpu.VMEM((5, PLANE, 64, TOK), BF16),
-            arrived, arrived, arrived, arrived, arrived, arrived, arrived, arrived,
+            arrived, arrived, arrived, pltpu.VMEM((8, 4, 2, 2, 16, TOK), F32), arrived, arrived, arrived, arrived, arrived,
             pltpu.VMEM((4, 4, 2, 2, 16, TOK), BF16),
             pltpu.VMEM((3, 8) + square, F32),
             pltpu.VMEM((4,) + square, F32),
-            pltpu.VMEM((4, 32, SIZE), F32),
+            pltpu.VMEM((2, 2, 32, SIZE), F32),
             pltpu.VMEM((3, 2, 8, 4, 32, SIZE), BF16),
             pltpu.VMEM((3, 2, 8, 4, 32, SIZE), BF16),
-            pltpu.VMEM((2, 7, 4, 32, SIZE), BF16),
-            pltpu.VMEM((2, 7, 4, 32, SIZE), BF16),
+            pltpu.VMEM((2, 7, 2, 2, 32, SIZE), BF16),
+            pltpu.VMEM((2, 7, 2, 2, 32, SIZE), BF16),
             dma((2,)), dma((2,)), dma((5,)), dma((5,)), dma((2, 8)),
-            dma((2, 24)), dma((2, 24)), dma((3, 2, 8)), dma((3, 2, 8)), dma((2, 7)), dma((2, 7)),
+            dma((2, 24)), dma((2, 24)), dma((3, 2, 8)), dma((3, 2, 8)), dma((2, 7, 2)), dma((2, 7, 2)),
         ],
         compiler_params=pltpu.CompilerParams(
             collective_id=0, has_side_effects=True, vmem_limit_bytes=56 << 20

time: 201 us -> 196 us (0.975); the launches traced: 199 us -> 196 us
  Pallas kernels: 193 us -> 190 us
    pallas_call x1, Pallas kernels: 193 us -> 190 us  [per_device(): pl.pallas_call(kernel, name='monarch', out_shape=(jax.ShapeDtypeStruct(fe...]
where the time goes in v3:
time: 196 us
  Pallas kernels  190 us (97%)
  local copies, waits for them, and re-layouts  5.41 us (3%)
    pallas_call x1, Pallas kernels, per_device(): pl.pallas_call(kernel, name='monarch', out_shape=(jax.ShapeDtypeStruct(fe...  190 us
    unnamed x13, local copies, waits for them, and re-layouts  5.41 us

profile of v3, /device:TPU:6, one launch (start us, length us, event | category | flops | bytes accessed | tf_op | source)
XLA Modules:
  0.0 196.0 jit_solution(2597480938264316116)
XLA Ops:
  0.6 190.0 %monarch.1 = (bf16[256,1024]{1,0:T(8,128)(2,1)}, f32[32,4,256]{2,1,0:T(4,128)}, f32[32,4,256]{2,1,0:T(4,128)}, f32[32,4,256]{2,1,0:T(4,128)}, f32[32,4,256]{2,1,0:T(4,128)}) custom-call(bf16[256,1024]{1,0:T(8,128)(2,1)} %feat_in.1, bf16[256,1024]{1,0:T(8,128)(2,1)} %cot_in.1, bf16[4,256,256]{2,1,0:T(8,128)(2,1)} %l1_in.1, bf16[4,256,256]{2,1,0:T(8,128)(2,1)} %r1_in.1, ...), custom_call_target="tpu_custom_call" | custom-call | flops 4000000000 | bytes 5000000 | tf_op jit(solution)/shard_map/monarch/pallas_call | solution.py:509
  190.6 0.0 copy-start.3
  190.6 1.9 copy.16
  192.5 0.0 copy-done.3
  192.5 0.0 copy-start.2
  192.5 0.7 copy.17
  193.2 0.3 copy-done.2
  193.5 0.0 copy-start.1
  193.5 0.7 copy.18
  194.1 0.3 copy-done.1
  194.4 0.0 copy-start
  194.4 0.7 copy.19
  195.1 0.3 copy-done
  195.4 0.7 copy.20
Async XLA Ops:
  190.6 1.9 copy-start.3
  192.5 1.0 copy-start.2
  193.5 1.0 copy-start.1
  194.4 1.0 copy-start
